TPU v7x, 256 devices: a whole 4x4x8 slice. The times are simulated.
256 devices in a mesh: slide: 8 (over x, core), seq: 32 (over y, z).
Axes of the slice: x: 4, y: 4, z: 8, core: 2. Of those that a mesh axis runs over, the one named last changes fastest.
Arguments:
- queries: bfloat16 [8, 8192, 1536], P('slide', 'seq'), may hold values from -9 to 9
- key_rows: bfloat16 [8, 8192, 1536], P('slide', 'seq'), may hold values from -9 to 9
- value_rows: bfloat16 [8, 8192, 1536], P('slide', 'seq'), may hold values from -12 to 12
- tissue: int32 [8, 8192], P('slide', 'seq'), may hold values from 0 to 1, as said below
- segment_len: int32 [24], replicated, may hold values from 128 to 256, as said below
- dilation: int32 [24], replicated, may hold values from 1 to 4, as said below
- out_weight: bfloat16 [1536, 1536], P(('slide', 'seq')), may hold values from -0.15625 to 0.15625
- grad_out: bfloat16 [8, 8192, 1536], P('slide', 'seq'), may hold values from -6 to 6
Outputs:
- layer_out: bfloat16 [8, 8192, 1536], P('slide', 'seq')
- grad_query: bfloat16 [8, 8192, 1536], P('slide', 'seq')
- grad_key: bfloat16 [8, 8192, 1536], P('slide', 'seq')
- grad_value: bfloat16 [8, 8192, 1536], P('slide', 'seq')
- grad_weight: float32 [1536, 1536], P(('slide', 'seq'))
Inputs may be any that keep to these rules, and one draw needn't show every extreme that they name: 1 for tissue, 0 for background. `segment_len`: each entry is 256 or 128, and each value is taken by some head. `dilation`: each entry is 1, 2 or 4; some head has 1 and some head 4.
All inputs are finite; a program needn't handle non-finite values.
Results may differ from a plain program's by a relative error of at most 0.0079.
Values may be sent and summed in bfloat16 or wider, within the bound.
A program may use at most 128 MiB of HBM per device.

v0:
```python
import functools
import math

import jax
import jax.numpy as jnp
from jax import lax
from jax.experimental import pallas as pl
from jax.experimental.pallas import tpu as pltpu
from jax.sharding import PartitionSpec as P

HD = 64
PAIR = 2 * HD
NX, NC, NY, NZ = 4, 2, 4, 8
NS = NY * NZ
TILES = 256
WIDTH = 1536
EACH = TILES // NS
PAIRS = WIDTH // PAIR
CH = 3
CW = WIDTH // CH
HW = CW // 2
CP = PAIRS // CH
LINE = WIDTH // (NX * NC)
BLOCK = LINE // NY
ROWS = BLOCK // NZ
CHUNKS = WIDTH // PAIR
PACK = 80
FLAG = 100.0
LOG2E = 1.4426950408889634
SCALE = HD**-0.5
NONE = -1e30
FLOOR = -1e29
MESH = pl.DeviceIdType.MESH
F32 = jnp.float32
BF16 = jnp.bfloat16
A_QK, A_V, A_O, A_G, A_GV, A_L, A_S = (CH * n for n in range(7))
A_GO = 7 * CH
A_ALL = 7 * CH + 1
SLOTS = PAIR // EACH


def nt(a, b):
    return lax.dot_general(a, b, (((1,), (1,)), ((), ())), preferred_element_type=F32)


def nn(a, b):
    return lax.dot_general(a, b, (((1,), (0,)), ((), ())), preferred_element_type=F32)


def tn(a, b):
    return lax.dot_general(a, b, (((0,), (0,)), ((), ())), preferred_element_type=F32)


def doubled(value):
    high = value.astype(BF16)
    return jnp.concatenate([high, (value - high.astype(F32)).astype(BF16)], axis=1)


def tripled(value):
    high = value.astype(BF16)
    rest = value - high.astype(F32)
    middle = rest.astype(BF16)
    return jnp.concatenate([high, middle, (rest - middle.astype(F32)).astype(BF16)], axis=1)


def slot_lane(lane):
    slot = lax.rem(lane, SLOTS)
    inner = lax.rem(slot, SLOTS // 2)
    return lax.div(inner, 2) + HD * lax.rem(inner, 2) + 16 * lax.div(slot, SLOTS // 2)


def own_slots():
    shape = (TILES, PAIR)
    return lax.div(iota(shape, 1), SLOTS) == lax.rem(iota(shape, 0), EACH)


def folded(stats):
    tall = (3 * PAIR, PAIR)
    move = (lax.rem(iota(tall, 0), PAIR) == slot_lane(iota(tall, 1))).astype(F32).astype(BF16)
    spread = jnp.where(own_slots(), nn(tripled(stats), move), 0.0)
    return jnp.sum(spread.reshape(NS, EACH, PAIR), axis=1, keepdims=True)


def unfolded(rows):
    tall = (3 * PAIR, PAIR)
    move = (slot_lane(lax.rem(iota(tall, 0), PAIR)) == iota(tall, 1)).astype(F32).astype(BF16)
    spread = jnp.broadcast_to(rows, (NS, EACH, PAIR)).reshape(TILES, PAIR)
    return nn(tripled(jnp.where(own_slots(), spread, 0.0)), move)


def iota(shape, axis):
    return lax.broadcasted_iota(jnp.int32, shape, axis)


def halves():
    low = (iota((1, PAIR), 1) < HD).astype(F32)
    return low.astype(BF16), (1.0 - low).astype(BF16)


def joined(a, b):
    shape = (NS, EACH, a.shape[1])
    both = [a.astype(F32).reshape(shape), b.astype(F32).reshape(shape)]
    return jnp.concatenate(both, axis=1).astype(BF16)


def parted(block):
    wide = block.astype(F32)
    shape = (TILES, block.shape[2])
    return wide[:, :EACH].reshape(shape).astype(BF16), wide[:, EACH:].reshape(shape).astype(BF16)


def unfold():
    line = iota((CHUNKS * BLOCK, PAIR), 0)
    inner = lax.rem(line, BLOCK)
    want = lax.div(inner, ROWS) * PACK + lax.div(line, BLOCK) * ROWS + lax.rem(inner, ROWS)
    lane = iota((CHUNKS * BLOCK, PAIR), 1)
    parts = [(lane + PAIR * n == want).astype(F32).astype(BF16) for n in range(NZ * PACK // PAIR)]
    return jnp.concatenate(parts, axis=1)


def stacked(value):
    return jnp.concatenate([value[:, n * PAIR : (n + 1) * PAIR] for n in range(CHUNKS)], axis=0)


def pair_at(p):
    return pl.ds(pl.multiple_of(p * PAIR, PAIR), PAIR)


def forward_pair(q, k, v, masked):
    ones = halves()
    tops, sums = [], []
    for e in range(2):
        scores = masked(e, nt(q * ones[e], k) * (SCALE * LOG2E))
        top = jnp.maximum(jnp.max(scores, axis=1, keepdims=True), FLOOR)
        weights = jnp.exp2(scores - top).astype(BF16)
        tops.append(top)
        sums.append(nn(weights, v * ones[e] + ones[1 - e]))
    low = iota((TILES, PAIR), 1) < HD
    total = pltpu.roll(jnp.where(low, sums[1], sums[0]), HD, 1)
    total = jnp.maximum(total, 1e-30)
    out = jnp.where(low, sums[0], sums[1]) / total
    lse = jnp.where(low, tops[0], tops[1]) + jnp.log(total) * LOG2E
    return out, lse


def backward_pair(q, k, v, d, masked, lse, delta):
    ones = halves()
    gq = gk = gv = None
    for e in range(2):
        qe, de, ke = q * ones[e], d * ones[e], k * ones[e]
        probs = masked(e, nt(k, qe) * (SCALE * LOG2E) - lse[e])
        dscore = (probs * (nt(v, de) - delta[e])).astype(BF16)
        terms = (tn(dscore, ke), nn(dscore, qe), nn(probs.astype(BF16), de))
        gq, gk, gv = terms if e == 0 else (gq + terms[0], gk + terms[1], gv + terms[2])
    return gq * SCALE, gk * SCALE, gv


def remote(src, dst, send, recv, peer):
    return pltpu.make_async_remote_copy(
        src_ref=src, dst_ref=dst, send_sem=send, recv_sem=recv, device_id=peer, device_id_type=MESH
    )


def kernel(
    factor,
    q_in, k_in, v_in, g_in, keep_in, seg, dil, w_in,
    out_lo, out_q, out_k, out_v, out_w,
    qp, kp, vp, gp, dp, qf, kf, vf, gf, df, of, o_near, attn, attn_t, nq, nk, nv,
    x_fwd, x_bwd, stat, stat_t, far_t, bias_row, bias_col,
    qk_s, v_s, gv_s, qk_r, v_r, o_r, g_r, gv_r, go_s, go_r,
    l_s, l_r, s_s, s_r,
    w_pad, w_src, w_z, w_full,
    c_s, c_r, own, x_s, x_r, y_s, y_r, z_s, z_r,
    a_send, a_recv, w_send, wz_recv, wy_recv, wx_recv, wc_recv,
    r_send, rc_recv, rx_recv, ry_recv, rz_recv,
):
    slide = lax.axis_index("slide")
    me = lax.axis_index("seq")
    x, c = lax.div(slide, NC), lax.rem(slide, NC)
    y, z = lax.div(me, NZ), lax.rem(me, NZ)

    def device(xx, cc, yy, zz):
        return (xx * NC + cc, yy * NZ + zz)

    def peer_of(n):
        return lax.rem(y + lax.div(n, NZ), NY) * NZ + lax.rem(z + lax.rem(n, NZ), NZ)

    sibling = device(x, 1 - c, y, z)
    barrier = pltpu.get_barrier_semaphore()

    def greet(n, carry):
        pl.semaphore_signal(barrier, inc=1, device_id=(slide, peer_of(n)), device_id_type=MESH)
        return carry

    lax.fori_loop(1, NS, greet, 0)
    for peer in [sibling] + [device(lax.rem(x + step, NX), c, y, z) for step in range(1, NX)]:
        pl.semaphore_signal(barrier, inc=1, device_id=peer, device_id_type=MESH)

    def exchange(src, dst, k):
        def body(n, carry):
            peer = peer_of(n)
            remote(src.at[peer], dst.at[me], a_send.at[k], a_recv.at[k], (slide, peer)).start()
            return carry

        lax.fori_loop(1, NS, body, 0)
        dst.at[me][...] = src.at[me][...]

    def arrived(dst, k):
        part = dst.at[pl.ds(0, NS - 1)]
        pltpu.make_async_copy(part, part, a_recv.at[k]).wait()

    def departed(src, k):
        part = src.at[pl.ds(0, NS - 1)]
        pltpu.make_async_copy(part, part, a_send.at[k]).wait()

    w_started, r_started = [], []

    def send_w(src, dst, recv, peer):
        copy = remote(src, dst, w_send.at[len(w_started)], recv, peer)
        copy.start()
        w_started.append(copy)
        return copy

    def send_r(src, dst, recv, peer):
        copy = remote(src, dst, r_send.at[len(r_started)], recv, peer)
        copy.start()
        r_started.append(copy)
        return copy

    def line_of(xx, cc):
        return pl.ds(pl.multiple_of((xx * NC + cc) * LINE, 16), LINE)

    square = (TILES, TILES)
    line, lane = iota(square, 0), iota(square, 1)
    order = (lane == lax.rem(line, EACH) * NS + lax.div(line, EACH)).astype(F32).astype(BF16)
    keep = keep_in[...].astype(F32).astype(BF16)
    keep_cols = nt(order, jnp.broadcast_to(keep, (PAIR, TILES)))
    keep_wide = jnp.concatenate([keep_cols] * (CW // PAIR), axis=1) > 0.5
    for ch in range(CH):
        cols = pl.ds(ch * CW, CW)
        q = nn(order, q_in[:, cols])
        k = nn(order, k_in[:, cols])
        qk_s[ch] = joined(q, jnp.where(keep_wide, k, FLAG))
        if ch == 0:
            pl.semaphore_wait(barrier, NS - 1 + NX)
        exchange(qk_s.at[ch], qk_r.at[ch], A_QK + ch)
        if ch == 0:
            w_pad[...] = jnp.zeros_like(w_pad)
            w_pad[0:ROWS, :] = w_in[...]
            out_row, in_row = iota((PACK, CHUNKS * 16), 0), iota((PACK, CHUNKS * 16), 1)
            chosen = (lax.div(out_row, ROWS) == lax.div(in_row, 16)) & (lax.rem(out_row, ROWS) == lax.rem(in_row, 16))
            w_src[...] = nn(chosen.astype(F32).astype(BF16), stacked(w_pad[...])).astype(BF16)
            w_z[z] = w_src[...]
            wz = [
                send_w(w_src, w_z.at[z], wz_recv.at[step - 1], device(x, c, y, lax.rem(z + step, NZ)))
                for step in range(1, NZ)
            ]
        qp[:, cols] = q.astype(BF16)
        kp[:, cols] = k.astype(BF16)
        v = nn(order, v_in[:, cols])
        v_s[ch] = joined(v[:, :HW], v[:, HW:])
        exchange(v_s.at[ch], v_r.at[ch], A_V + ch)
        vp[:, cols] = v.astype(BF16)
        if ch == 0:
            half = WIDTH // 2
            ends = []
            for cols in (pl.ds(0, half), pl.ds(half, half)):
                ends.append(nn(order, g_in[:, cols]))
                gp[:, cols] = ends[-1].astype(BF16)
            go_s[...] = joined(*ends)
            exchange(go_s, go_r, A_GO)

    keep_row = nt(jnp.broadcast_to(keep, (16, TILES)), order)[0:1]
    pos_l = lax.rem(line, EACH) * NS + lax.div(line, EACH)
    pos_c = lax.rem(lane, EACH) * NS + lax.div(lane, EACH)
    apart = lax.bitwise_xor(pos_l, pos_c)
    same = line == lane
    x_fwd[...] = jnp.where(same, 0, apart + jnp.where(keep_row > 0.5, 0, 65536))
    x_bwd[...] = jnp.where(same, 0, apart + jnp.where(keep_wide[:, :TILES], 0, 65536))

    def bits(p, e):
        head = 2 * p + e
        return 65536 + (TILES - seg[head]) + (dil[head] - 1)

    for copy in wz:
        copy.wait_recv()
    mine = pl.ds(pl.multiple_of(((x * NC + c) * NY + y) * BLOCK, 16), BLOCK)
    rows = nn(unfold(), w_z[...].reshape(NZ * PACK, PAIR)).astype(BF16)
    for n in range(CHUNKS):
        w_full[mine, n * PAIR : (n + 1) * PAIR] = rows[n * BLOCK : (n + 1) * BLOCK]
    wy = [
        send_w(w_full.at[mine], w_full.at[mine], wy_recv.at[step - 1], device(x, c, lax.rem(y + step, NY), z))
        for step in range(1, NY)
    ]

    def put_stat(p, stats, values):
        return jnp.where(lax.rem(iota((TILES, PAIR), 1), HD) == p, values, stats)

    def near_forward(ch, p, stats):
        at = pair_at(p)

        def masked(e, scores):
            return jnp.where(lax.bitwise_and(x_fwd[...], bits(p, e)) == 0, scores, NONE)

        out, lse = forward_pair(qp[:, at], kp[:, at], vp[:, at], masked)
        o_near[:, at] = out
        return put_stat(p - ch * CP, stats, lse)

    def near_chunk(ch):
        empty = jnp.zeros((TILES, PAIR), F32)
        stat[ch] = lax.fori_loop(ch * CP, (ch + 1) * CP, functools.partial(near_forward, ch), empty)

    near_chunk(0)

    for copy in wy:
        copy.wait_recv()
    mine = line_of(x, c)
    wx = [
        send_w(w_full.at[mine], w_full.at[mine], wx_recv.at[step - 1], device(lax.rem(x + step, NX), c, y, z))
        for step in range(1, NX)
    ]
    wc = [send_w(w_full.at[mine], w_full.at[mine], wc_recv.at[0], sibling)]
    for ch in range(1, CH):
        near_chunk(ch)

    def columns(ch):
        return pl.ds(ch * CW, CW), pl.ds(ch * CW, HW), pl.ds(ch * CW + HW, HW)

    def far_forward(ch, p, stats):
        at = pair_at(p)
        out, lse = forward_pair(
            qf[:, at], kf[:, at], vf[:, at], lambda e, scores: scores + bias_row[0:1, :]
        )
        of[:, at] = out.astype(BF16)
        return put_stat(p - ch * CP, stats, lse)

    def far_chunk(ch):
        cols, low, high = columns(ch)
        arrived(qk_r.at[ch], A_QK + ch)
        qf[:, cols], kf[:, cols] = parted(qk_r[ch])
        if ch == 0:
            bias = jnp.where(kf[:, 0:PAIR].astype(F32) > FLAG / 2, NONE, 0.0)
            bias_col[...] = jnp.concatenate([bias, bias], axis=1)
            bias_row[...] = jnp.transpose(bias)[0:8]
        arrived(v_r.at[ch], A_V + ch)
        vf[:, low], vf[:, high] = parted(v_r[ch])
        empty = jnp.zeros((TILES, PAIR), F32)
        lse = lax.fori_loop(ch * CP, (ch + 1) * CP, functools.partial(far_forward, ch), empty)
        departed(v_s.at[ch], A_V + ch)
        v_s[ch] = joined(of[:, low], of[:, high])
        exchange(v_s.at[ch], o_r.at[ch], A_O + ch)
        l_s[ch] = folded(lse)
        exchange(l_s.at[ch], l_r.at[ch], A_L + ch)

    def combine(ch, share_near, share_far, p, delta):
        at = pair_at(p)
        near = p - ch * CP
        tall = (2 * PAIR, PAIR)
        first, second = lax.rem(iota(tall, 0), PAIR), iota(tall, 1)
        together = (first < HD) == (second < HD)
        spread = (together & (lax.rem(first, HD) == near)).astype(F32).astype(BF16)
        gather = (together & (lax.rem(second, HD) == near + 16)).astype(F32).astype(BF16)
        far = of[:, at].astype(F32)
        whole = nn(share_near, spread) * o_near[:, at] + nn(share_far, spread) * far
        attn[:, at] = whole.astype(BF16)
        attn_t[at, :] = jnp.transpose(whole).astype(BF16)
        return delta + nn(doubled(whole * dp[:, at].astype(F32)), gather)

    def combine_chunk(ch):
        cols, low, high = columns(ch)
        arrived(l_r.at[ch], A_L + ch)
        lse_near = stat[ch]
        lse_far = unfolded(l_r[ch])
        top = jnp.maximum(lse_near, lse_far)
        lse = top + jnp.log(jnp.exp2(lse_near - top) + jnp.exp2(lse_far - top)) * LOG2E
        share_near = doubled(jnp.exp2(lse_near - lse))
        share_far = doubled(jnp.exp2(lse_far - lse))
        arrived(o_r.at[ch], A_O + ch)
        of[:, low], of[:, high] = parted(o_r[ch])
        body = functools.partial(combine, ch, share_near, share_far)
        delta = lax.fori_loop(ch * CP, (ch + 1) * CP, body, jnp.zeros((TILES, PAIR), F32))
        stats = jnp.where(lax.rem(iota((TILES, PAIR), 1), HD) < 16, lse, delta)
        s_s[ch] = folded(stats)
        exchange(s_s.at[ch], s_r.at[ch], A_S + ch)
        stat_t[ch] = jnp.transpose(stats)

    def rows_of(table, p):
        lse = [table[pl.ds(p + HD * e, 1), :] for e in range(2)]
        delta = [table[pl.ds(p + HD * e + 16, 1), :] for e in range(2)]
        return lse, delta

    def far_backward(ch, p, carry):
        at = pair_at(p)
        here = pair_at(p - ch * CP)
        gq, gk, gv = backward_pair(
            qf[:, at], kf[:, at], vf[:, at], df[:, at],
            lambda e, scores: jnp.exp2(scores + bias_col[...]), *rows_of(far_t, p - ch * CP),
        )
        qk_s[ch, :, :, here] = joined(gq, gk)
        vf[:, at] = gv.astype(BF16)
        return carry

    def back_chunk(ch):
        cols, low, high = columns(ch)
        arrived(s_r.at[ch], A_S + ch)
        far_t[...] = jnp.transpose(unfolded(s_r[ch]))
        departed(qk_s.at[ch], A_QK + ch)
        lax.fori_loop(ch * CP, (ch + 1) * CP, functools.partial(far_backward, ch), 0)
        exchange(qk_s.at[ch], g_r.at[ch], A_G + ch)
        gv_s[ch] = joined(vf[:, low], vf[:, high])
        exchange(gv_s.at[ch], gv_r.at[ch], A_GV + ch)

    far_chunk(0)
    for step in range(1, NX):
        wx[step - 1].wait_recv()
        there = line_of(lax.rem(x + NX - step, NX), c)
        wc.append(send_w(w_full.at[there], w_full.at[there], wc_recv.at[step], sibling))
    for copy in wc:
        copy.wait_recv()
    arrived(go_r, A_GO)
    gf[:, : WIDTH // 2], gf[:, WIDTH // 2 :] = parted(go_r[...])
    for ch in range(CH):
        cols = pl.ds(ch * CW, CW)
        dp[:, cols] = nt(gp[...], w_full[cols, :]).astype(BF16)
        df[:, cols] = nt(gf[...], w_full[cols, :]).astype(BF16)
    for ch in range(1, CH):
        far_chunk(ch)
        combine_chunk(ch - 1)
    back_chunk(0)
    combine_chunk(CH - 1)

    for step in range(NX):
        to = lax.rem(x + step + 1, NX)
        c_s[step] = nn(attn_t[line_of(to, 1 - c), :], gp[...]).astype(BF16)
        send_r(c_s.at[step], c_r.at[step], rc_recv.at[step], sibling)
    for ch in range(1, CH - 1):
        back_chunk(ch)

    ahead = []
    for step in range(NX):
        to = lax.rem(x + step + 1, NX)
        r_started[step].wait_recv()
        total = nn(attn_t[line_of(to, c), :], gp[...]) + c_r[step].astype(F32)
        if step < NX - 1:
            x_s[step] = total.astype(BF16)
            ahead.append(send_r(x_s.at[step], x_r.at[step], rx_recv.at[step], device(to, c, y, z)))
        else:
            own[...] = total
    back_chunk(CH - 1)

    def near_backward(ch, p, carry):
        at = pair_at(p)

        def masked(e, scores):
            return jnp.where(lax.bitwise_and(x_bwd[...], bits(p, e)) == 0, jnp.exp2(scores), 0.0)

        nq[:, at], nk[:, at], nv[:, at] = backward_pair(
            qp[:, at], kp[:, at], vp[:, at], dp[:, at], masked, *rows_of(stat_t.at[ch], p - ch * CP)
        )
        return carry

    def near_back_chunk(ch):
        lax.fori_loop(ch * CP, (ch + 1) * CP, functools.partial(near_backward, ch), 0)

    near_back_chunk(0)
    for copy in ahead:
        copy.wait_recv()
    total = own[...]
    for step in range(NX - 1):
        total = total + x_r[step].astype(F32)
    y_s[...] = total.reshape(NY, BLOCK, WIDTH)
    ahead = []
    for step in range(NY - 1):
        to = lax.rem(y + step + 1, NY)
        ahead.append(send_r(y_s.at[to], y_r.at[step], ry_recv.at[step], device(x, c, to, z)))
    for ch in range(1, CH):
        near_back_chunk(ch)
    for copy in ahead:
        copy.wait_recv()
    total = y_s[y]
    for step in range(NY - 1):
        total = total + y_r[step]
    z_s[...] = tn(unfold(), stacked(total).astype(BF16)).astype(BF16).reshape(NZ, PACK, PAIR)
    ahead = []
    for step in range(NZ - 1):
        to = lax.rem(z + step + 1, NZ)
        ahead.append(send_r(z_s.at[to], z_r.at[step], rz_recv.at[step], device(x, c, y, to)))

    for ch in range(CH):
        cols = pl.ds(ch * CW, CW)
        done = nn(attn[...], w_full[:, cols]).astype(BF16)
        out_lo[:, cols] = done

    for ch in range(CH):
        cols, low, high = pl.ds(ch * CW, CW), pl.ds(ch * CW, HW), pl.ds(ch * CW + HW, HW)
        arrived(g_r.at[ch], A_G + ch)
        far_q, far_k = parted(g_r[ch])
        out_q[:, cols] = (nq[:, cols] + far_q.astype(F32)).astype(BF16)
        out_k[:, cols] = (nk[:, cols] + far_k.astype(F32)).astype(BF16)
        arrived(gv_r.at[ch], A_GV + ch)
        far_low, far_high = parted(gv_r[ch])
        out_v[:, low] = (nv[:, low] + far_low.astype(F32)).astype(BF16)
        out_v[:, high] = (nv[:, high] + far_high.astype(F32)).astype(BF16)

    for copy in ahead:
        copy.wait_recv()
    total = z_s[z].astype(F32)
    for step in range(NZ - 1):
        total = total + z_r[step].astype(F32)
    for n in range(CHUNKS):
        out_w[:, n * PAIR : (n + 1) * PAIR] = total[n * ROWS : (n + 1) * ROWS] * factor
    for copy in w_started + r_started:
        copy.wait_send()
    for ch in range(CH):
        departed(v_s.at[ch], A_O + ch)
        departed(qk_s.at[ch], A_G + ch)
        departed(gv_s.at[ch], A_GV + ch)
        departed(l_s.at[ch], A_L + ch)
        departed(s_s.at[ch], A_S + ch)
    departed(go_s, A_GO)


def reorder(*refs):
    square = (TILES, TILES)
    line, lane = iota(square, 0), iota(square, 1)
    back = (lane == lax.rem(line, NS) * EACH + lax.div(line, NS)).astype(F32).astype(BF16)
    for src, dst in zip(refs[:4], refs[4:]):
        dst[...] = nn(back, src[...]).astype(BF16)


def natural(rows):
    wide = WIDTH // 2
    block = pl.BlockSpec((TILES, wide), lambda n: (0, n))
    return pl.pallas_call(
        reorder,
        grid=(WIDTH // wide,),
        out_shape=[jax.ShapeDtypeStruct((TILES, WIDTH), BF16)] * 4,
        in_specs=[block] * 4,
        out_specs=[block] * 4,
    )(*rows)


def layer(queries, key_rows, value_rows, tissue, segment_len, dilation, out_weight, grad_out):
    shape = (TILES, WIDTH)
    vmem = pl.BlockSpec(memory_space=pltpu.VMEM)
    smem = pl.BlockSpec(memory_space=pltpu.SMEM)
    low, wide = pltpu.VMEM(shape, BF16), pltpu.VMEM(shape, F32)
    stats = pltpu.VMEM((CH, NS, 1, PAIR), F32)
    table = pltpu.VMEM((PAIR, TILES), F32)
    square = pltpu.VMEM((TILES, TILES), jnp.int32)
    both = pltpu.VMEM((CH, NS, 2 * EACH, CW), BF16)
    single = pltpu.VMEM((CH, NS, 2 * EACH, HW), BF16)
    ends = pltpu.VMEM((NS, 2 * EACH, WIDTH // 2), BF16)
    dma = pltpu.SemaphoreType.DMA
    factor = 1.0 / math.sqrt(NX * NC * NS * TILES)
    outs = pl.pallas_call(
        functools.partial(kernel, factor),
        out_shape=[jax.ShapeDtypeStruct(shape, BF16)] * 4 + [jax.ShapeDtypeStruct((ROWS, WIDTH), F32)],
        in_specs=[vmem] * 5 + [smem] * 2 + [vmem],
        out_specs=[vmem] * 5,
        scratch_shapes=[low] * 11 + [wide] + [low, pltpu.VMEM((WIDTH, TILES), BF16)] + [wide] * 3
        + [square] * 2 + [pltpu.VMEM((CH, TILES, PAIR), F32), pltpu.VMEM((CH, PAIR, TILES), F32), table]
        + [pltpu.VMEM((8, TILES), F32), pltpu.VMEM((TILES, TILES), F32)]
        + [both, single, single, both, single, single, both, single, ends, ends]
        + [stats] * 4
        + [
            pltpu.VMEM((16, WIDTH), BF16),
            pltpu.VMEM((PACK, PAIR), BF16),
            pltpu.VMEM((NZ, PACK, PAIR), BF16),
            pltpu.VMEM((WIDTH, WIDTH), BF16),
            pltpu.VMEM((NX, LINE, WIDTH), BF16),
            pltpu.VMEM((NX, LINE, WIDTH), BF16),
            pltpu.VMEM((LINE, WIDTH), F32),
            pltpu.VMEM((NX - 1, LINE, WIDTH), BF16),
            pltpu.VMEM((NX - 1, LINE, WIDTH), BF16),
            pltpu.VMEM((NY, BLOCK, WIDTH), F32),
            pltpu.VMEM((NY - 1, BLOCK, WIDTH), F32),
            pltpu.VMEM((NZ, PACK, PAIR), BF16),
            pltpu.VMEM((NZ - 1, PACK, PAIR), BF16),
            dma((A_ALL,)),
            dma((A_ALL,)),
            dma((NZ + NY + 2 * NX,)),
            dma((NZ,)),
            dma((NY,)),
            dma((NX,)),
            dma((NX,)),
            dma((NZ + NY + 2 * NX,)),
            dma((NX,)),
            dma((NX,)),
            dma((NY,)),
            dma((NZ,)),
        ],
        compiler_params=pltpu.CompilerParams(
            collective_id=0, has_side_effects=True, vmem_limit_bytes=60 * 1024 * 1024
        ),
    )(
        queries[0], key_rows[0], value_rows[0], grad_out[0], tissue, segment_len, dilation, out_weight
    )
    return tuple(out[None] for out in natural(outs[:4])) + (outs[4],)


def solution(mesh):
    tiles = P("slide", "seq", None)
    rows = P(("slide", "seq"), None)
    return jax.shard_map(
        layer,
        mesh=mesh,
        in_specs=(tiles, tiles, tiles, P("slide", "seq"), P(), P(), rows, tiles),
        out_specs=(tiles, tiles, tiles, tiles, rows),
        check_vma=False,
    )
```

profile of v0, /device:TPU:2, one launch (start us, length us, event | category | flops | bytes accessed | tf_op | source)
XLA Modules:
  0.0 178.4 jit_solution(10292139371028316983)
XLA Ops:
  0.6 173.7 %shard_map.119 = (bf16[256,1536]{1,0:T(8,128)(2,1)}, bf16[256,1536]{1,0:T(8,128)(2,1)}, bf16[256,1536]{1,0:T(8,128)(2,1)}, bf16[256,1536]{1,0:T(8,128)(2,1)}, f32[6,1536]{1,0:T(8,128)}) custom-call(bf16[256,1536]{1,0:T(8,128)(2,1)} %bitcast.8, bf16[256,1536]{1,0:T(8,128)(2,1)} %bitcast.9, bf16[256,1536]{1,0:T(8,128)(2,1)} %bitcast.10, ...), custom_call_target="tpu_custom_call" | custom-call | tf_op jit(solution)/shard_map/pallas_call | solution.py:556
  174.3 0.0 copy-start
  174.3 3.4 %shard_map.120 = (bf16[256,1536]{1,0:T(8,128)(2,1)}, bf16[256,1536]{1,0:T(8,128)(2,1)}, bf16[256,1536]{1,0:T(8,128)(2,1)}, bf16[256,1536]{1,0:T(8,128)(2,1)}) custom-call(bf16[256,1536]{1,0:T(8,128)(2,1)} %get-tuple-element.14.refs_0_, bf16[256,1536]{1,0:T(8,128)(2,1)} %get-tuple-element.15.refs_1_, bf16[256,1536]{1,0:T(8,128)(2,1)} %get-tuple-element.16.refs_2_, ...), custom_call_target="tpu_custom_call" | custom-call | tf_op jit(solution)/shard_map/pallas_call | solution.py:534
  177.7 0.0 copy-done
  177.7 0.6 copy.14
Async XLA Ops:
  174.3 3.4 %copy-start = (f32[6,1536]{1,0:T(8,128)S(1)}, f32[6,1536]{1,0:T(8,128)}, u32[]{:S(2)}) copy-start(f32[6,1536]{1,0:T(8,128)} %get-tuple-element.32) | copy-start | bytes 110596
where the time goes:
time: 178 us
  Pallas kernels  177 us (99%)
    pallas_call x1, Pallas kernels, layer(): pl.pallas_call(functools.partial(kernel, factor), out_shape=[jax.ShapeDty...  174 us

commit v1 on v0

--- a/solution.py
+++ b/solution.py
@@ -33,9 +33,9 @@
 MESH = pl.DeviceIdType.MESH
 F32 = jnp.float32
 BF16 = jnp.bfloat16
-A_QK, A_V, A_O, A_G, A_GV, A_L, A_S = (CH * n for n in range(7))
-A_GO = 7 * CH
-A_ALL = 7 * CH + 1
+A_QK, A_O, A_G, A_L, A_S = (CH * n for n in range(5))
+A_GO = 5 * CH
+A_ALL = 5 * CH + 1
 SLOTS = PAIR // EACH
 
 
@@ -167,7 +167,7 @@
     out_lo, out_q, out_k, out_v, out_w,
     qp, kp, vp, gp, dp, qf, kf, vf, gf, df, of, o_near, attn, attn_t, nq, nk, nv,
     x_fwd, x_bwd, stat, stat_t, far_t, bias_row, bias_col,
-    qk_s, v_s, gv_s, qk_r, v_r, o_r, g_r, gv_r, go_s, go_r,
+    qk_s, v_s, qk_r, o_r, g_r, go_s, go_r,
     l_s, l_r, s_s, s_r,
     w_pad, w_src, w_z, w_full,
     c_s, c_r, own, x_s, x_r, y_s, y_r, z_s, z_r,
@@ -240,7 +240,9 @@
         cols = pl.ds(ch * CW, CW)
         q = nn(order, q_in[:, cols])
         k = nn(order, k_in[:, cols])
-        qk_s[ch] = joined(q, jnp.where(keep_wide, k, FLAG))
+        qk_s[ch, :, :, 0:CW] = joined(q, jnp.where(keep_wide, k, FLAG))
+        v = nn(order, v_in[:, cols])
+        qk_s[ch, :, :, CW:] = joined(v[:, :HW], v[:, HW:])
         if ch == 0:
             pl.semaphore_wait(barrier, NS - 1 + NX)
         exchange(qk_s.at[ch], qk_r.at[ch], A_QK + ch)
@@ -257,9 +259,6 @@
             ]
         qp[:, cols] = q.astype(BF16)
         kp[:, cols] = k.astype(BF16)
-        v = nn(order, v_in[:, cols])
-        v_s[ch] = joined(v[:, :HW], v[:, HW:])
-        exchange(v_s.at[ch], v_r.at[ch], A_V + ch)
         vp[:, cols] = v.astype(BF16)
         if ch == 0:
             half = WIDTH // 2
@@ -337,16 +336,14 @@
     def far_chunk(ch):
         cols, low, high = columns(ch)
         arrived(qk_r.at[ch], A_QK + ch)
-        qf[:, cols], kf[:, cols] = parted(qk_r[ch])
+        qf[:, cols], kf[:, cols] = parted(qk_r[ch, :, :, 0:CW])
         if ch == 0:
             bias = jnp.where(kf[:, 0:PAIR].astype(F32) > FLAG / 2, NONE, 0.0)
             bias_col[...] = jnp.concatenate([bias, bias], axis=1)
             bias_row[...] = jnp.transpose(bias)[0:8]
-        arrived(v_r.at[ch], A_V + ch)
-        vf[:, low], vf[:, high] = parted(v_r[ch])
+        vf[:, low], vf[:, high] = parted(qk_r[ch, :, :, CW:])
         empty = jnp.zeros((TILES, PAIR), F32)
         lse = lax.fori_loop(ch * CP, (ch + 1) * CP, functools.partial(far_forward, ch), empty)
-        departed(v_s.at[ch], A_V + ch)
         v_s[ch] = joined(of[:, low], of[:, high])
         exchange(v_s.at[ch], o_r.at[ch], A_O + ch)
         l_s[ch] = folded(lse)
@@ -406,15 +403,15 @@
         far_t[...] = jnp.transpose(unfolded(s_r[ch]))
         departed(qk_s.at[ch], A_QK + ch)
         lax.fori_loop(ch * CP, (ch + 1) * CP, functools.partial(far_backward, ch), 0)
+        qk_s[ch, :, :, CW:] = joined(vf[:, low], vf[:, high])
         exchange(qk_s.at[ch], g_r.at[ch], A_G + ch)
-        gv_s[ch] = joined(vf[:, low], vf[:, high])
-        exchange(gv_s.at[ch], gv_r.at[ch], A_GV + ch)
 
     far_chunk(0)
     for step in range(1, NX):
         wx[step - 1].wait_recv()
         there = line_of(lax.rem(x + NX - step, NX), c)
         wc.append(send_w(w_full.at[there], w_full.at[there], wc_recv.at[step], sibling))
+    far_chunk(1)
     for copy in wc:
         copy.wait_recv()
     arrived(go_r, A_GO)
@@ -423,7 +420,8 @@
         cols = pl.ds(ch * CW, CW)
         dp[:, cols] = nt(gp[...], w_full[cols, :]).astype(BF16)
         df[:, cols] = nt(gf[...], w_full[cols, :]).astype(BF16)
-    for ch in range(1, CH):
+    combine_chunk(0)
+    for ch in range(2, CH):
         far_chunk(ch)
         combine_chunk(ch - 1)
     back_chunk(0)
@@ -494,11 +492,10 @@
     for ch in range(CH):
         cols, low, high = pl.ds(ch * CW, CW), pl.ds(ch * CW, HW), pl.ds(ch * CW + HW, HW)
         arrived(g_r.at[ch], A_G + ch)
-        far_q, far_k = parted(g_r[ch])
+        far_q, far_k = parted(g_r[ch, :, :, 0:CW])
         out_q[:, cols] = (nq[:, cols] + far_q.astype(F32)).astype(BF16)
         out_k[:, cols] = (nk[:, cols] + far_k.astype(F32)).astype(BF16)
-        arrived(gv_r.at[ch], A_GV + ch)
-        far_low, far_high = parted(gv_r[ch])
+        far_low, far_high = parted(g_r[ch, :, :, CW:])
         out_v[:, low] = (nv[:, low] + far_low.astype(F32)).astype(BF16)
         out_v[:, high] = (nv[:, high] + far_high.astype(F32)).astype(BF16)
 
@@ -514,7 +511,6 @@
     for ch in range(CH):
         departed(v_s.at[ch], A_O + ch)
         departed(qk_s.at[ch], A_G + ch)
-        departed(gv_s.at[ch], A_GV + ch)
         departed(l_s.at[ch], A_L + ch)
         departed(s_s.at[ch], A_S + ch)
     departed(go_s, A_GO)
@@ -548,7 +544,7 @@
     stats = pltpu.VMEM((CH, NS, 1, PAIR), F32)
     table = pltpu.VMEM((PAIR, TILES), F32)
     square = pltpu.VMEM((TILES, TILES), jnp.int32)
-    both = pltpu.VMEM((CH, NS, 2 * EACH, CW), BF16)
+    three = pltpu.VMEM((CH, NS, 2 * EACH, CW + HW), BF16)
     single = pltpu.VMEM((CH, NS, 2 * EACH, HW), BF16)
     ends = pltpu.VMEM((NS, 2 * EACH, WIDTH // 2), BF16)
     dma = pltpu.SemaphoreType.DMA
@@ -561,7 +557,7 @@
         scratch_shapes=[low] * 11 + [wide] + [low, pltpu.VMEM((WIDTH, TILES), BF16)] + [wide] * 3
         + [square] * 2 + [pltpu.VMEM((CH, TILES, PAIR), F32), pltpu.VMEM((CH, PAIR, TILES), F32), table]
         + [pltpu.VMEM((8, TILES), F32), pltpu.VMEM((TILES, TILES), F32)]
-        + [both, single, single, both, single, single, both, single, ends, ends]
+        + [three, single, three, single, three, ends, ends]
         + [stats] * 4
         + [
             pltpu.VMEM((16, WIDTH), BF16),

time: 178 us -> 179 us (level)
  no operation moved by 1% of the time
where the time goes in v1:
time: 179 us
  Pallas kernels  177 us (99%)
    pallas_call x1, Pallas kernels, layer(): pl.pallas_call(functools.partial(kernel, factor), out_shape=[jax.ShapeDty...  174 us

profile of v1, /device:TPU:2, one launch (start us, length us, event | category | flops | bytes accessed | tf_op | source)
XLA Modules:
  0.0 178.8 jit_solution(4865400420033891073)
XLA Ops:
  0.6 174.1 %shard_map.119 = (bf16[256,1536]{1,0:T(8,128)(2,1)}, bf16[256,1536]{1,0:T(8,128)(2,1)}, bf16[256,1536]{1,0:T(8,128)(2,1)}, bf16[256,1536]{1,0:T(8,128)(2,1)}, f32[6,1536]{1,0:T(8,128)}) custom-call(bf16[256,1536]{1,0:T(8,128)(2,1)} %bitcast.8, bf16[256,1536]{1,0:T(8,128)(2,1)} %bitcast.9, bf16[256,1536]{1,0:T(8,128)(2,1)} %bitcast.10, ...), custom_call_target="tpu_custom_call" | custom-call | tf_op jit(solution)/shard_map/pallas_call | solution.py:552
  174.7 0.0 copy-start
  174.7 3.4 %shard_map.120 = (bf16[256,1536]{1,0:T(8,128)(2,1)}, bf16[256,1536]{1,0:T(8,128)(2,1)}, bf16[256,1536]{1,0:T(8,128)(2,1)}, bf16[256,1536]{1,0:T(8,128)(2,1)}) custom-call(bf16[256,1536]{1,0:T(8,128)(2,1)} %get-tuple-element.14.refs_0_, bf16[256,1536]{1,0:T(8,128)(2,1)} %get-tuple-element.15.refs_1_, bf16[256,1536]{1,0:T(8,128)(2,1)} %get-tuple-element.16.refs_2_, ...), custom_call_target="tpu_custom_call" | custom-call | tf_op jit(solution)/shard_map/pallas_call | solution.py:530
  178.1 0.0 copy-done
  178.2 0.6 copy.14
Async XLA Ops:
  174.7 3.4 %copy-start = (f32[6,1536]{1,0:T(8,128)S(1)}, f32[6,1536]{1,0:T(8,128)}, u32[]{:S(2)}) copy-start(f32[6,1536]{1,0:T(8,128)} %get-tuple-element.32) | copy-start | bytes 110596

commit v2 on v0

--- a/solution.py
+++ b/solution.py
@@ -243,8 +243,8 @@
         qk_s[ch] = joined(q, jnp.where(keep_wide, k, FLAG))
         if ch == 0:
             pl.semaphore_wait(barrier, NS - 1 + NX)
-        exchange(qk_s.at[ch], qk_r.at[ch], A_QK + ch)
         if ch == 0:
+            exchange(qk_s.at[ch], qk_r.at[ch], A_QK + ch)
             w_pad[...] = jnp.zeros_like(w_pad)
             w_pad[0:ROWS, :] = w_in[...]
             out_row, in_row = iota((PACK, CHUNKS * 16), 0), iota((PACK, CHUNKS * 16), 1)
@@ -259,7 +259,8 @@
         kp[:, cols] = k.astype(BF16)
         v = nn(order, v_in[:, cols])
         v_s[ch] = joined(v[:, :HW], v[:, HW:])
-        exchange(v_s.at[ch], v_r.at[ch], A_V + ch)
+        if ch == 0:
+            exchange(v_s.at[ch], v_r.at[ch], A_V + ch)
         vp[:, cols] = v.astype(BF16)
         if ch == 0:
             half = WIDTH // 2
@@ -310,7 +311,12 @@
         empty = jnp.zeros((TILES, PAIR), F32)
         stat[ch] = lax.fori_loop(ch * CP, (ch + 1) * CP, functools.partial(near_forward, ch), empty)
 
+    def send_chunk(ch):
+        exchange(qk_s.at[ch], qk_r.at[ch], A_QK + ch)
+        exchange(v_s.at[ch], v_r.at[ch], A_V + ch)
+
     near_chunk(0)
+    send_chunk(1)
 
     for copy in wy:
         copy.wait_recv()
@@ -322,6 +328,8 @@
     wc = [send_w(w_full.at[mine], w_full.at[mine], wc_recv.at[0], sibling)]
     for ch in range(1, CH):
         near_chunk(ch)
+    for ch in range(2, CH):
+        send_chunk(ch)
 
     def columns(ch):
         return pl.ds(ch * CW, CW), pl.ds(ch * CW, HW), pl.ds(ch * CW + HW, HW)
@@ -468,7 +476,7 @@
     total = own[...]
     for step in range(NX - 1):
         total = total + x_r[step].astype(F32)
-    y_s[...] = total.reshape(NY, BLOCK, WIDTH)
+    y_s[...] = total.reshape(NY, BLOCK, WIDTH).astype(BF16)
     ahead = []
     for step in range(NY - 1):
         to = lax.rem(y + step + 1, NY)
@@ -477,9 +485,9 @@
         near_back_chunk(ch)
     for copy in ahead:
         copy.wait_recv()
-    total = y_s[y]
+    total = y_s[y].astype(F32)
     for step in range(NY - 1):
-        total = total + y_r[step]
+        total = total + y_r[step].astype(F32)
     z_s[...] = tn(unfold(), stacked(total).astype(BF16)).astype(BF16).reshape(NZ, PACK, PAIR)
     ahead = []
     for step in range(NZ - 1):
@@ -573,8 +581,8 @@
             pltpu.VMEM((LINE, WIDTH), F32),
             pltpu.VMEM((NX - 1, LINE, WIDTH), BF16),
             pltpu.VMEM((NX - 1, LINE, WIDTH), BF16),
-            pltpu.VMEM((NY, BLOCK, WIDTH), F32),
-            pltpu.VMEM((NY - 1, BLOCK, WIDTH), F32),
+            pltpu.VMEM((NY, BLOCK, WIDTH), BF16),
+            pltpu.VMEM((NY - 1, BLOCK, WIDTH), BF16),
             pltpu.VMEM((NZ, PACK, PAIR), BF16),
             pltpu.VMEM((NZ - 1, PACK, PAIR), BF16),
             dma((A_ALL,)),

time: 178 us -> 172 us (0.966)
  Pallas kernels: 177 us -> 170 us
    pallas_call x1, Pallas kernels: 174 us -> 167 us  [layer(): pl.pallas_call(functools.partial(kernel, factor), out_shape=[jax.ShapeDty...]
where the time goes in v2:
time: 172 us
  Pallas kernels  170 us (99%)
    pallas_call x1, Pallas kernels, layer(): pl.pallas_call(functools.partial(kernel, factor), out_shape=[jax.ShapeDty...  167 us

profile of v2, /device:TPU:2, one launch (start us, length us, event | category | flops | bytes accessed | tf_op | source)
XLA Modules:
  0.0 171.6 jit_solution(12284864638824657465)
XLA Ops:
  0.6 166.9 %shard_map.119 = (bf16[256,1536]{1,0:T(8,128)(2,1)}, bf16[256,1536]{1,0:T(8,128)(2,1)}, bf16[256,1536]{1,0:T(8,128)(2,1)}, bf16[256,1536]{1,0:T(8,128)(2,1)}, f32[6,1536]{1,0:T(8,128)}) custom-call(bf16[256,1536]{1,0:T(8,128)(2,1)} %bitcast.8, bf16[256,1536]{1,0:T(8,128)(2,1)} %bitcast.9, bf16[256,1536]{1,0:T(8,128)(2,1)} %bitcast.10, ...), custom_call_target="tpu_custom_call" | custom-call | tf_op jit(solution)/shard_map/pallas_call | solution.py:564
  167.5 0.0 copy-start
  167.6 3.4 %shard_map.120 = (bf16[256,1536]{1,0:T(8,128)(2,1)}, bf16[256,1536]{1,0:T(8,128)(2,1)}, bf16[256,1536]{1,0:T(8,128)(2,1)}, bf16[256,1536]{1,0:T(8,128)(2,1)}) custom-call(bf16[256,1536]{1,0:T(8,128)(2,1)} %get-tuple-element.14.refs_0_, bf16[256,1536]{1,0:T(8,128)(2,1)} %get-tuple-element.15.refs_1_, bf16[256,1536]{1,0:T(8,128)(2,1)} %get-tuple-element.16.refs_2_, ...), custom_call_target="tpu_custom_call" | custom-call | tf_op jit(solution)/shard_map/pallas_call | solution.py:542
  171.0 0.0 copy-done
  171.0 0.6 copy.14
Async XLA Ops:
  167.5 3.4 %copy-start = (f32[6,1536]{1,0:T(8,128)S(1)}, f32[6,1536]{1,0:T(8,128)}, u32[]{:S(2)}) copy-start(f32[6,1536]{1,0:T(8,128)} %get-tuple-element.32) | copy-start | bytes 110596
